TPU v7x, 32 devices: a whole 2x2x4 slice. The times are simulated.
32 devices in a mesh: groups: 2 (over y), seq: 4 (over z), head: 4 (over x, core).
Axes of the slice: x: 2, y: 2, z: 4, core: 2. Of those that a mesh axis runs over, the one named last changes fastest.
Arguments:
- query: bfloat16 [16, 1024, 128], P('head', ('groups', 'seq')), parts along dimension 1, may hold values from -400 to 400
- keys: bfloat16 [4, 1024, 128], P('head', ('groups', 'seq')), parts along dimension 1, may hold values from -5 to 5
- values: bfloat16 [4, 1024, 128], P('head', ('groups', 'seq')), parts along dimension 1, may hold values from -6 to 6
- ratio: bfloat16 [16, 1024, 128], P('head', ('groups', 'seq')), parts along dimension 1, may hold values from -4 to 4
- block_order: int32 [16], P('groups'), parts along dimension 0, may hold values from 0 to 7, each once
Outputs:
- query_rel: float32 [16, 1024, 128], P('head', ('groups', 'seq')), parts along dimension 1
- key_rel: float32 [4, 1024, 128], P('head', ('groups', 'seq')), parts along dimension 1
- value_rel: float32 [4, 1024, 128], P('head', ('groups', 'seq')), parts along dimension 1
There are 2 independent parts, one for each index of `groups`. A program takes and returns all parts, laid end to end along the dimension named above; each array names one. Nothing has to cross between parts.
Inputs may be any that keep to these rules, and one draw needn't show every extreme that they name: A permutation: stored block b holds prompt block block_order[b], each once.
All inputs are finite; a program needn't handle non-finite values.
Results may differ from a plain program's by a relative error of at most 0.04.
Values may be sent and summed in bfloat16 or wider, within the bound.
A program may use at most 64 MiB of HBM per device.

v0:
```python
import math

import jax
import jax.numpy as jnp
from jax import lax
from jax.sharding import PartitionSpec as P


def block_width(row_total):
    return math.gcd(row_total, 512)


def token_places(block_order, block_rows):
    offsets = jnp.arange(block_rows, dtype=jnp.int32)
    return (block_order[:, None] * block_rows + offsets[None, :]).reshape(-1)


def scores_of(query_rows, query_places, key_block, key_places, score_scale):
    scores = (
        jnp.einsum("qd,kd->qk", query_rows, key_block, preferred_element_type=jnp.float32)
        * score_scale
    )
    return jnp.where(key_places[None, :] <= query_places[:, None], scores, -jnp.inf)


def row_stats(query_rows, ratio_rows, query_places, key_all, value_all, key_places, score_scale):
    block_size = block_width(key_all.shape[0])
    row_count = query_rows.shape[0]

    def row_advance(step_index, loop_state):
        first_row = step_index * block_size
        key_block = lax.dynamic_slice_in_dim(key_all, first_row, block_size, 0)
        value_block = lax.dynamic_slice_in_dim(value_all, first_row, block_size, 0)
        block_places = lax.dynamic_slice_in_dim(key_places, first_row, block_size, 0)
        row_top, row_total, weighted = loop_state
        scores = scores_of(query_rows, query_places, key_block, block_places, score_scale)
        new_top = jnp.maximum(row_top, jnp.max(scores, axis=1))
        shrink = jnp.exp(row_top - new_top)
        exp_scores = jnp.exp(scores - new_top[:, None])
        prob_grad = jnp.einsum(
            "qd,kd->qk", ratio_rows, value_block, preferred_element_type=jnp.float32
        )
        return (
            new_top,
            row_total * shrink + jnp.sum(exp_scores, axis=1),
            weighted * shrink + jnp.sum(exp_scores * prob_grad, axis=1),
        )

    start_state = (
        jnp.full((row_count,), -1e30, jnp.float32),
        jnp.zeros((row_count,), jnp.float32),
        jnp.zeros((row_count,), jnp.float32),
    )
    row_top, row_total, weighted = lax.fori_loop(
        0, key_all.shape[0] // block_size, row_advance, start_state
    )
    return (row_top, row_total, weighted / row_total)


def block_grads(
    query_rows, ratio_rows, query_places, stats, key_block, value_block, key_places, score_scale
):
    row_top, row_total, row_expect = stats
    scores = scores_of(query_rows, query_places, key_block, key_places, score_scale)
    weights = jnp.exp(scores - row_top[:, None]) / row_total[:, None]
    prob_grad = jnp.einsum("qd,kd->qk", ratio_rows, value_block, preferred_element_type=jnp.float32)
    soft_grad = (weights * (prob_grad - row_expect[:, None])).astype(jnp.bfloat16)
    return (soft_grad, weights.astype(jnp.bfloat16))


def side_terms(soft_grad, low_weights, query_rows, ratio_rows):
    key_part = jnp.einsum("qk,qd->kd", soft_grad, query_rows, preferred_element_type=jnp.float32)
    value_part = jnp.einsum(
        "qk,qd->kd", low_weights, ratio_rows, preferred_element_type=jnp.float32
    )
    return jnp.concatenate((key_part, value_part), axis=1)


def query_pass(
    query_rows, ratio_rows, query_places, stats, key_all, value_all, key_places, score_scale
):
    block_size = block_width(key_all.shape[0])
    head_size = key_all.shape[1]

    def query_advance(step_index, loop_state):
        first_row = step_index * block_size
        key_block = lax.dynamic_slice_in_dim(key_all, first_row, block_size, 0)
        value_block = lax.dynamic_slice_in_dim(value_all, first_row, block_size, 0)
        block_places = lax.dynamic_slice_in_dim(key_places, first_row, block_size, 0)
        query_sum, term_table = loop_state
        soft_grad, low_weights = block_grads(
            query_rows,
            ratio_rows,
            query_places,
            stats,
            key_block,
            value_block,
            block_places,
            score_scale,
        )
        query_sum = query_sum + jnp.dot(soft_grad, key_block, preferred_element_type=jnp.float32)
        pieces = side_terms(soft_grad, low_weights, query_rows, ratio_rows)
        term_table = lax.dynamic_update_slice_in_dim(term_table, pieces, first_row, 0)
        return (query_sum, term_table)

    empty_table = jnp.zeros((key_all.shape[0], 2 * head_size), jnp.float32)
    start_state = (jnp.zeros((query_rows.shape[0], head_size), jnp.float32), empty_table)
    return lax.fori_loop(0, key_all.shape[0] // block_size, query_advance, start_state)


def body(query, keys, values, ratio, block_order):
    kv_heads, tokens_dev, head_size = keys.shape
    group_size = query.shape[0] // kv_heads
    score_scale = head_size ** (-0.5)
    places_all = token_places(block_order, tokens_dev // 2)
    seq_index = lax.axis_index("seq")
    local_places = lax.dynamic_slice_in_dim(places_all, seq_index * tokens_dev, tokens_dev, 0)
    row_places = jnp.tile(local_places, group_size)
    key_all, value_all = (
        lax.all_gather(keys, "seq", axis=1, tiled=True),
        lax.all_gather(values, "seq", axis=1, tiled=True),
    )
    query_list, key_list, value_list = ([], [], [])
    query_rows = query.reshape(group_size * tokens_dev, head_size)
    ratio_rows = ratio.reshape(group_size * tokens_dev, head_size)
    keys_seen = key_all[0]
    values_seen = value_all[0]
    stats = row_stats(
        query_rows, ratio_rows, row_places, keys_seen, values_seen, places_all, score_scale
    )
    query_sum, term_table = query_pass(
        query_rows, ratio_rows, row_places, stats, keys_seen, values_seen, places_all, score_scale
    )

    def term_rows(first_row, row_count, table=term_table):
        return table

    summed = lax.psum_scatter(
        term_rows(jnp.int32(0), lax.axis_size("seq") * tokens_dev),
        "seq",
        scatter_dimension=0,
        tiled=True,
    )
    query_list.append(
        0.5
        * score_scale
        * query.astype(jnp.float32)
        * query_sum.reshape(group_size, tokens_dev, head_size)
    )
    key_list.append(0.5 * score_scale * keys[0].astype(jnp.float32) * summed[:, :head_size])
    value_list.append(values[0].astype(jnp.float32) * summed[:, head_size:])
    return (query_list[0], jnp.stack(key_list, axis=0), jnp.stack(value_list, axis=0))


def solution(mesh):
    return jax.shard_map(
        body,
        mesh=mesh,
        in_specs=(
            P("head", ("groups", "seq"), None),
            P("head", ("groups", "seq"), None),
            P("head", ("groups", "seq"), None),
            P("head", ("groups", "seq"), None),
            P("groups"),
        ),
        out_specs=(
            P("head", ("groups", "seq"), None),
            P("head", ("groups", "seq"), None),
            P("head", ("groups", "seq"), None),
        ),
        check_vma=False,
    )
```

profile of v0, /device:TPU:0, one launch (start us, length us, event | category | flops | bytes accessed | tf_op | source)
XLA Modules:
  0.0 71.7 jit_solution(825619412379754486)
XLA Ops:
  7.2 0.0 copy-start
  7.2 0.0 copy-start.1
  7.2 0.0 reduce-scatter.2.cloned.1.call-start
  7.2 0.0 copy-start.4
  7.2 15.4 %all_gather.6 = bf16[1,512,128]{2,1,0:T(8,128)(2,1)S(1)} all-gather(bf16[1,128,128]{2,1,0:T(8,128)(2,1)} %param.6), channel_id=1, replica_groups=mesh['groups'=2,'seq'=4,'head'=4] {'seq'}, dimensions={1}, use_global_device_ids=true | all-gather | bytes 163840 | tf_op jit(solution)/shard_map/all_gather | solution.py:120
  22.7 0.0 copy-done.4
  22.7 0.1 iota_add_fusion
  22.7 0.1 add.67
  22.8 0.1 dynamic_slice.15
  22.9 0.0 copy-done.1
  22.9 0.0 copy-start.2
  22.9 0.4 fusion.13
  23.3 0.4 copy-done.2
  23.7 13.5 %all_gather.7 = bf16[1,512,128]{2,1,0:T(8,128)(2,1)S(1)} all-gather(bf16[1,128,128]{2,1,0:T(8,128)(2,1)S(1)} %copy-done.2), channel_id=1, replica_groups=mesh['groups'=2,'seq'=4,'head'=4] {'seq'}, dimensions={1}, use_global_device_ids=true | all-gather | bytes 163840 | tf_op jit(solution)/shard_map/all_gather | solution.py:121
  37.2 0.0 copy-done
  37.2 0.4 fusion.2
  37.6 0.4 fusion.3
  38.1 0.3 multiply_convert_fusion
  38.4 0.3 fusion.14
  38.7 0.8 %pad_maximum_fusion = f32[512,256]{0,1:T(8,128)} fusion(f32[512,128]{0,1:T(8,128)S(1)} %fusion.3, f32[512,128]{0,1:T(8,128)S(1)} %fusion.14), kind=kLoop, calls=%fused_computation.8 | loop fusion | flops 131072 | bytes 1048576 | tf_op jit(solution)/shard_map/while/body/eval_jaxpr/concatenate | solution.py:76
  39.5 0.0 reduce-scatter.2.cloned.1.call-update
  39.5 0.0 copy-start.3
  39.5 0.1 copy.9
  39.6 0.6 copy-done.3
  40.3 0.1 copy.8
  40.4 1.0 %convolution_multiply_fusion.1 = f32[4,128,128]{2,1,0:T(8,128)} fusion(bf16[4,128,512]{2,1,0:T(8,128)(2,1)S(1)} %bitcast.35, bf16[4,128,128]{2,1,0:T(8,128)(2,1)S(1)} %copy-done.1, bf16[1,512,128]{2,1,0:T(8,128)(2,1)S(1)} %all_gather.6), kind=kOutput, calls=%fused_computation.2 | convolution fusion | flops 67305472 | bytes 1048576 | tf_op jit(solution)/shard_map/while/body/eval_jaxpr/dot_general | solution.py:101
  41.4 21.1 %reduce-scatter.2.cloned.1.call-done = f32[128,256]{0,1:T(8,128)} async-done(((f32[512,256]{0,1:T(8,128)}), f32[128,256]{0,1:T(8,128)}) %reduce-scatter.2.cloned.1.call-update) | async-done | bytes 131088 | tf_op jit(solution)/shard_map/reduce_scatter | solution.py:138
  62.5 0.9 %fusion.9 = (f32[1,128,128]{1,2,0:T(8,128)S(1)}, f32[1,128,128]{1,2,0:T(8,128)S(1)}) fusion(f32[128,256]{0,1:T(8,128)} %reduce-scatter.2.cloned.1.call-done, bf16[1,128,128]{1,2,0:T(8,128)(2,1)S(1)} %copy.9, bf16[1,128,128]{1,2,0:T(8,128)(2,1)S(1)} %copy.8), kind=kLoop, calls=%fused_computation.16 | loop fusion | flops 81920 | bytes 327680 | tf_op jit(solution)/shard_map/stack | solution.py:152
  63.4 0.7 %copy.10 = f32[1,128,128]{2,1,0:T(8,128)} copy(f32[1,128,128]{1,2,0:T(8,128)S(1)} %get-tuple-element.55) | data formatting | bytes 131072
  64.1 0.7 %copy.11 = f32[1,128,128]{2,1,0:T(8,128)} copy(f32[1,128,128]{1,2,0:T(8,128)S(1)} %get-tuple-element.54) | data formatting | bytes 131072
  (4 shorter events, 0.0 us)
Async XLA Ops:
  7.2 30.0 %copy-start = (bf16[4,128,128]{2,1,0:T(8,128)(2,1)S(1)}, bf16[4,128,128]{2,1,0:T(8,128)(2,1)}, u32[]{:S(2)}) copy-start(bf16[4,128,128]{2,1,0:T(8,128)(2,1)} %param.8) | copy-start | bytes 393220
  7.2 15.7 %copy-start.1 = (bf16[4,128,128]{2,1,0:T(8,128)(2,1)S(1)}, bf16[4,128,128]{2,1,0:T(8,128)(2,1)}, u32[]{:S(2)}) copy-start(bf16[4,128,128]{2,1,0:T(8,128)(2,1)} %param.5) | copy-start | bytes 393220
  7.2 55.3 %reduce-scatter.2.cloned.1.call-start = ((), (), s32[]{:S(2)}) async-start(), calls=%async_computation.1 | async-start | bytes 655360 | tf_op jit(solution)/shard_map/reduce_scatter | solution.py:138
  7.2 15.4 %copy-start.4 = (s32[8]{0:T(128)S(1)}, s32[8]{0:T(128)}, u32[]{:S(2)}) copy-start(s32[8]{0:T(128)} %param.9) | copy-start | bytes 100
  22.9 0.8 %copy-start.2 = (bf16[1,128,128]{2,1,0:T(8,128)(2,1)S(1)}, bf16[1,128,128]{2,1,0:T(8,128)(2,1)}, u32[]{:S(2)}) copy-start(bf16[1,128,128]{2,1,0:T(8,128)(2,1)} %param.7) | copy-start | bytes 98308
  39.5 0.8 %copy-start.3 = (bf16[1,128,128]{2,1,0:T(8,128)(2,1)S(1)}, bf16[1,128,128]{2,1,0:T(8,128)(2,1)}, u32[]{:S(2)}) copy-start(bf16[1,128,128]{2,1,0:T(8,128)(2,1)} %param.6) | copy-start | bytes 98308
Sparse Core Ops, SparseCore 0:
  39.6 22.8 reduce-scatter.1
where the time goes:
time: 72 us; the launch traced here: 71.7 us
  blocking collectives  28.9 us (40%)
  waiting for transfers between devices  21.1 us (29%)
  between operations  14.1 us (20%)
  local copies, waits for them, and re-layouts  2.85 us (4%)
  matrix products  2.54 us (4%)
  other arithmetic  2.12 us (3%)
    reduce_scatter x1, waiting for transfers between devices, body(): lax.psum_scatter(term_rows(jnp.int32(0), lax.axis_size('seq') * tokens_de...  21.1 us
    all_gather x1, blocking collectives, body(): lax.all_gather(keys, 'seq', axis=1, tiled=True)  15.4 us
    all_gather x1, blocking collectives, body(): lax.all_gather(values, 'seq', axis=1, tiled=True)  13.5 us
    unnamed x14, local copies, waits for them, and re-layouts  2.69 us
  transfers between devices with their start and end apart: 1, of which 1 were waited for; matrix products, arithmetic and copies ran while one was open for 2% of the time, Pallas kernels for 0%

commit v1 on v0

v1 whole, which is shorter than its diff:
```python
import functools
import math

import jax
import jax.numpy as jnp
from jax import lax
from jax.experimental import pallas as pl
from jax.experimental.pallas import tpu as pltpu
from jax.sharding import PartitionSpec as P

MESH = pl.DeviceIdType.MESH
MASKED = -1e30
NT = (((1,), (1,)), ((), ()))
TN = (((0,), (0,)), ((), ()))


def dot(a, b, dims=None):
    if dims is None:
        return jnp.dot(a, b, preferred_element_type=jnp.float32)
    return lax.dot_general(a, b, dims, preferred_element_type=jnp.float32)


def each(first, last, step):
    if last - first <= 8:
        for i in range(first, last):
            step(i)
    else:
        pl.loop(first, last)(step)


def kernel(
    n,
    order_ref,
    query_hbm,
    keys_hbm,
    values_hbm,
    ratio_hbm,
    query_rel,
    key_rel,
    value_rel,
    query,
    ratio,
    kbuf,
    vbuf,
    exps,
    grads,
    tops,
    sums,
    low,
    soft,
    dv_out,
    dk_out,
    dv_in,
    dk_in,
    local_sem,
    k_send,
    k_recv,
    v_send,
    v_recv,
    dv_send,
    dv_recv,
    dk_send,
    dk_recv,
):
    heads, rows, depth = query_hbm.shape
    wide = heads * rows
    scale = depth**-0.5
    rate = scale * math.log2(math.e)
    per_device = order_ref.shape[0] // n
    block_rows = rows // per_device
    me = lax.axis_index("seq")

    def to(d):
        return {"seq": lax.rem(me + d, n)}

    def back(d):
        return {"seq": lax.rem(me + n - d, n)}

    loads = [
        pltpu.make_async_copy(keys_hbm.at[0], kbuf.at[0], local_sem.at[0]),
        pltpu.make_async_copy(query_hbm, query, local_sem.at[1]),
        pltpu.make_async_copy(ratio_hbm, ratio, local_sem.at[2]),
        pltpu.make_async_copy(values_hbm.at[0], vbuf.at[0], local_sem.at[3]),
    ]
    for load in loads:
        load.start()

    barrier = pltpu.get_barrier_semaphore()

    def greet(d):
        pl.semaphore_signal(barrier, inc=1, device_id=to(d), device_id_type=MESH)

    each(1, n, greet)
    pl.semaphore_wait(barrier, n - 1)

    def k_copy(d):
        return pltpu.make_async_remote_copy(
            src_ref=keys_hbm.at[0],
            dst_ref=kbuf.at[d],
            send_sem=k_send.at[d],
            recv_sem=k_recv.at[d],
            device_id=to(d),
            device_id_type=MESH,
        )

    def v_copy(d):
        return pltpu.make_async_remote_copy(
            src_ref=values_hbm.at[0],
            dst_ref=vbuf.at[d],
            send_sem=v_send.at[d],
            recv_sem=v_recv.at[d],
            device_id=to(d),
            device_id_type=MESH,
        )

    def dv_copy(d):
        return pltpu.make_async_remote_copy(
            src_ref=dv_out.at[d],
            dst_ref=dv_in.at[d],
            send_sem=dv_send.at[d],
            recv_sem=dv_recv.at[d],
            device_id=back(d),
            device_id_type=MESH,
        )

    def dk_copy(d):
        return pltpu.make_async_remote_copy(
            src_ref=dk_out.at[d],
            dst_ref=dk_in.at[d],
            send_sem=dk_send.at[d],
            recv_sem=dk_recv.at[d],
            device_id=back(d),
            device_id_type=MESH,
        )

    each(1, n, lambda d: k_copy(d).start())
    each(1, n, lambda d: v_copy(d).start())

    def places(owner, axis):
        index = lax.broadcasted_iota(jnp.int32, (rows, rows), axis)
        within = lax.rem(index, block_rows)
        first = order_ref[owner * per_device] * block_rows
        for b in range(1, per_device):
            first = jnp.where(
                index >= b * block_rows, order_ref[owner * per_device + b] * block_rows, first
            )
        return first + within

    loads[0].wait()
    loads[1].wait()
    query_places = places(me, 1)

    def score_step(d):
        owner = lax.rem(me + n - d, n)
        bias = jnp.where(places(owner, 0) <= query_places, 0.0, MASKED)
        rows_in = query[...].reshape(wide, depth)
        scores = dot(kbuf[d], rows_in, NT) + jnp.concatenate([bias] * heads, axis=1)
        top = jnp.max(scores, axis=0, keepdims=True)
        e = jnp.exp2((scores - top) * rate)
        exps[d] = e
        tops[d] = top
        sums[d] = jnp.sum(e, axis=0, keepdims=True)

    score_step(0)
    loads[2].wait()
    loads[3].wait()

    def grad_step(d):
        grads[d] = dot(vbuf[d], ratio[...].reshape(wide, depth), NT)

    grad_step(0)

    def k_step(d):
        k_copy(d).wait_recv()
        score_step(d)

    each(1, n, k_step)

    top = jnp.max(tops[...], axis=0)
    total = jnp.sum(sums[...] * jnp.exp2((tops[...] - top) * rate), axis=0)
    inverse = 1.0 / total

    def weight_step(d):
        w = exps[d] * (jnp.exp2((tops[d] - top) * rate) * inverse)
        exps[d] = w
        low[d] = w.astype(jnp.bfloat16)

    def value_part(d):
        return dot(low[d], ratio[...].reshape(wide, depth))

    def dv_step(d):
        weight_step(d)
        dv_out[d] = value_part(d).astype(jnp.bfloat16)
        dv_copy(d).start()

    each(1, n, dv_step)
    weight_step(0)
    own_value = value_part(0)

    def v_step(d):
        v_copy(d).wait_recv()
        grad_step(d)

    each(1, n, v_step)

    if n <= 8:
        expect = sum(jnp.sum(exps[d] * grads[d], axis=0, keepdims=True) for d in range(n))
    else:
        expect = lax.fori_loop(
            0,
            n,
            lambda d, e: e + jnp.sum(exps[d] * grads[d], axis=0, keepdims=True),
            jnp.zeros((1, wide), jnp.float32),
        )

    def soft_step(d):
        soft[d] = (exps[d] * (grads[d] - expect)).astype(jnp.bfloat16)

    def key_part(d):
        return dot(soft[d], query[...].reshape(wide, depth))

    def dk_step(d):
        soft_step(d)
        dk_out[d] = key_part(d).astype(jnp.bfloat16)
        dk_copy(d).start()

    each(1, n, dk_step)
    soft_step(0)
    own_key = key_part(0)

    query_sum = dot(
        kbuf[...].reshape(n * rows, depth), soft[...].reshape(n * rows, wide), TN
    )
    for h in range(heads):
        query_rel[h] = (
            0.5
            * scale
            * query[h].astype(jnp.float32)
            * query_sum[:, h * rows : (h + 1) * rows].T
        )

    each(1, n, lambda d: dv_copy(d).wait_recv())
    value_rel[0] = vbuf[0].astype(jnp.float32) * (
        own_value + jnp.sum(dv_in[1:].astype(jnp.float32), axis=0)
    )
    each(1, n, lambda d: dk_copy(d).wait_recv())
    key_rel[0] = (
        0.5
        * scale
        * kbuf[0].astype(jnp.float32)
        * (own_key + jnp.sum(dk_in[1:].astype(jnp.float32), axis=0))
    )

    def drain(d):
        k_copy(d).wait_send()
        v_copy(d).wait_send()
        dv_copy(d).wait_send()
        dk_copy(d).wait_send()

    each(1, n, drain)


def body(n, query, keys, values, ratio, block_order):
    heads, rows, depth = query.shape
    wide = heads * rows
    bf16, f32 = jnp.bfloat16, jnp.float32
    anywhere = pl.BlockSpec(memory_space=pl.ANY)
    vmem = pl.BlockSpec(memory_space=pltpu.VMEM)
    dma = pltpu.SemaphoreType.DMA((n,))
    return pl.pallas_call(
        functools.partial(kernel, n),
        out_shape=[
            jax.ShapeDtypeStruct(query.shape, f32),
            jax.ShapeDtypeStruct(keys.shape, f32),
            jax.ShapeDtypeStruct(values.shape, f32),
        ],
        in_specs=[pl.BlockSpec(memory_space=pltpu.SMEM)] + [anywhere] * 4,
        out_specs=[vmem] * 3,
        scratch_shapes=[
            pltpu.VMEM((heads, rows, depth), bf16),
            pltpu.VMEM((heads, rows, depth), bf16),
            pltpu.VMEM((n, rows, depth), bf16),
            pltpu.VMEM((n, rows, depth), bf16),
            pltpu.VMEM((n, rows, wide), f32),
            pltpu.VMEM((n, rows, wide), f32),
            pltpu.VMEM((n, 1, wide), f32),
            pltpu.VMEM((n, 1, wide), f32),
            pltpu.VMEM((n, rows, wide), bf16),
            pltpu.VMEM((n, rows, wide), bf16),
            pltpu.VMEM((n, rows, depth), bf16),
            pltpu.VMEM((n, rows, depth), bf16),
            pltpu.VMEM((n, rows, depth), bf16),
            pltpu.VMEM((n, rows, depth), bf16),
            pltpu.SemaphoreType.DMA((4,)),
        ]
        + [dma] * 8,
        compiler_params=pltpu.CompilerParams(
            collective_id=0, has_side_effects=True, vmem_limit_bytes=56 * 2**20
        ),
    )(block_order, query, keys, values, ratio)


def solution(mesh):
    spec = P("head", ("groups", "seq"), None)
    return jax.shard_map(
        functools.partial(body, mesh.shape["seq"]),
        mesh=mesh,
        in_specs=(spec, spec, spec, spec, P("groups")),
        out_specs=(spec, spec, spec),
        check_vma=False,
    )
```

time: 72 us -> 24.5 us (0.34)
  blocking collectives: 28.9 us -> 0 us
  waiting for transfers between devices: 21.1 us -> 0 us
  Pallas kernels: 0 us -> 20.5 us
  between operations: 14.1 us -> 0.65 us
  matrix products: 2.54 us -> 0 us
  other arithmetic: 2.12 us -> 0 us
    all_gather x2 -> x0, blocking collectives: 28.9 us -> none  [the longest x1 15.4 us: body(): lax.all_gather(keys, 'seq', axis=1, tiled=True)]
    reduce_scatter x1 -> x0, waiting for transfers between devices: 21.1 us -> none  [body(): lax.psum_scatter(term_rows(jnp.int32(0), lax.axis_size('seq') * tokens_de...]
    pallas_call x0 -> x1, Pallas kernels: none -> 20.5 us  [body(): pl.pallas_call(functools.partial(kernel, n), out_shape=[jax.ShapeDtypeStr...]
    dot_general x5 -> x0, matrix products: 2.54 us -> none  [the longest x1 1.01 us: query_advance(): jnp.dot(soft_grad, key_block, preferred_element_type=jnp.float32)]
    another operation x1 -> x0, other arithmetic: 0.89 us -> none  [body(): jnp.stack(value_list, axis=0)]
    concatenate x1 -> x0, other arithmetic: 0.82 us -> none  [side_terms(): return jnp.concatenate((key_part, value_part), axis=1)]
    unnamed x14 -> x7, local copies, waits for them, and re-layouts: 2.69 us -> 3.2 us
  transfers between devices with their start and end apart: 1 -> 0, of which waited for: 1 -> 0; matrix products, arithmetic and copies ran while one was open for 2% -> 0% of each run, Pallas kernels for 0% -> 0%
where the time goes in v1:
time: 24.5 us; the launch traced here: 24.3 us
  Pallas kernels  20.5 us (84%)
  local copies, waits for them, and re-layouts  3.2 us (13%)
  between operations  0.65 us (3%)
    pallas_call x1, Pallas kernels, body(): pl.pallas_call(functools.partial(kernel, n), out_shape=[jax.ShapeDtypeStr...  20.5 us
    unnamed x7, local copies, waits for them, and re-layouts  3.2 us

profile of v1, /device:TPU:0, one launch (start us, length us, event | category | flops | bytes accessed | tf_op | source)
XLA Modules:
  0.0 24.3 jit_solution(17253797445687969474)
XLA Ops:
  0.6 20.5 %shard_map.76 = (f32[4,128,128]{2,1,0:T(8,128)}, f32[1,128,128]{2,1,0:T(8,128)}, f32[1,128,128]{2,1,0:T(8,128)}) custom-call(s32[8]{0:T(128)} %order_ref.1, bf16[4,128,128]{2,1,0:T(8,128)(2,1)} %query_hbm.1, bf16[1,128,128]{2,1,0:T(8,128)(2,1)} %keys_hbm.1, bf16[1,128,128]{2,1,0:T(8,128)(2,1)} %values_hbm.1, bf16[4,128,128]{2,1,0:T(8,128)(2,1)} %ratio_hbm.1), custom_call_target="tpu_custom_call" | custom-call | tf_op jit(solution)/shard_map/pallas_call | solution.py:270
  21.1 0.0 copy-start.1
  21.1 1.7 %copy.11 = f32[4,128,128]{2,1,0:T(8,128)} copy(f32[4,128,128]{2,1,0:T(8,128)} %get-tuple-element.6) | data formatting | bytes 524288
  22.8 0.0 copy-done.1
  22.8 0.0 copy-start
  22.8 0.6 %copy.12 = f32[1,128,128]{2,1,0:T(8,128)} copy(f32[1,128,128]{2,1,0:T(8,128)S(1)} %copy-done.1) | data formatting | bytes 131072
  23.5 0.2 copy-done
  23.7 0.6 %copy.13 = f32[1,128,128]{2,1,0:T(8,128)} copy(f32[1,128,128]{2,1,0:T(8,128)S(1)} %copy-done) | data formatting | bytes 131072
Async XLA Ops:
  21.1 1.7 %copy-start.1 = (f32[1,128,128]{2,1,0:T(8,128)S(1)}, f32[1,128,128]{2,1,0:T(8,128)}, u32[]{:S(2)}) copy-start(f32[1,128,128]{2,1,0:T(8,128)} %get-tuple-element.7) | copy-start | bytes 196612
  22.8 0.9 %copy-start = (f32[1,128,128]{2,1,0:T(8,128)S(1)}, f32[1,128,128]{2,1,0:T(8,128)}, u32[]{:S(2)}) copy-start(f32[1,128,128]{2,1,0:T(8,128)} %get-tuple-element.8) | copy-start | bytes 196612

commit v2 on v1

--- a/solution.py
+++ b/solution.py
@@ -270,9 +270,9 @@
     return pl.pallas_call(
         functools.partial(kernel, n),
         out_shape=[
-            jax.ShapeDtypeStruct(query.shape, f32),
-            jax.ShapeDtypeStruct(keys.shape, f32),
-            jax.ShapeDtypeStruct(values.shape, f32),
+            pltpu.VMEM(query.shape, f32),
+            pltpu.VMEM(keys.shape, f32),
+            pltpu.VMEM(values.shape, f32),
         ],
         in_specs=[pl.BlockSpec(memory_space=pltpu.SMEM)] + [anywhere] * 4,
         out_specs=[vmem] * 3,

time: 24.5 us -> 22.5 us (0.918)
  local copies, waits for them, and re-layouts: 3.2 us -> 1.96 us
  Pallas kernels: 20.5 us -> 19.7 us
    unnamed x7 -> x3, local copies, waits for them, and re-layouts: 3.2 us -> 1.96 us
    pallas_call x1, Pallas kernels: 20.5 us -> 19.7 us  [body(): pl.pallas_call(functools.partial(kernel, n), out_shape=[pltpu.VMEM(query....]
where the time goes in v2:
time: 22.5 us; the launch traced here: 22.3 us
  Pallas kernels  19.7 us (88%)
  local copies, waits for them, and re-layouts  1.96 us (9%)
  between operations  0.64 us (3%)
    pallas_call x1, Pallas kernels, body(): pl.pallas_call(functools.partial(kernel, n), out_shape=[pltpu.VMEM(query....  19.7 us
    unnamed x3, local copies, waits for them, and re-layouts  1.96 us

profile of v2, /device:TPU:0, one launch (start us, length us, event | category | flops | bytes accessed | tf_op | source)
XLA Modules:
  0.0 22.3 jit_solution(12980225274476002086)
XLA Ops:
  0.6 19.7 %shard_map.76 = (f32[4,128,128]{2,1,0:T(8,128)S(1)}, f32[1,128,128]{2,1,0:T(8,128)S(1)}, f32[1,128,128]{2,1,0:T(8,128)S(1)}) custom-call(s32[8]{0:T(128)} %order_ref.1, bf16[4,128,128]{2,1,0:T(8,128)(2,1)} %query_hbm.1, bf16[1,128,128]{2,1,0:T(8,128)(2,1)} %keys_hbm.1, bf16[1,128,128]{2,1,0:T(8,128)(2,1)} %values_hbm.1, bf16[4,128,128]{2,1,0:T(8,128)(2,1)} %ratio_hbm.1), custom_call_target="tpu_custom_call" | custom-call | tf_op jit(solution)/shard_map/pallas_call | solution.py:270
  20.4 0.7 %copy.11 = f32[4,128,128]{2,1,0:T(8,128)} copy(f32[4,128,128]{2,1,0:T(8,128)S(1)} %get-tuple-element.3) | data formatting | bytes 524288
  21.1 0.6 %copy.12 = f32[1,128,128]{2,1,0:T(8,128)} copy(f32[1,128,128]{2,1,0:T(8,128)S(1)} %get-tuple-element.4) | data formatting | bytes 131072
  21.7 0.6 %copy.13 = f32[1,128,128]{2,1,0:T(8,128)} copy(f32[1,128,128]{2,1,0:T(8,128)S(1)} %get-tuple-element.5) | data formatting | bytes 131072

commit v3 on v2

--- a/solution.py
+++ b/solution.py
@@ -70,11 +70,21 @@
     block_rows = rows // per_device
     me = lax.axis_index("seq")
 
+    pair = me + 1 - 2 * lax.rem(me, 2)
+
+    def peer(d, sign):
+        odd = d % 2
+        return lax.rem(me + (pair - me) * odd + n + sign * (d - odd), n)
+
     def to(d):
-        return {"seq": lax.rem(me + d, n)}
+        return {"seq": peer(d, 1)}
 
     def back(d):
-        return {"seq": lax.rem(me + n - d, n)}
+        return {"seq": peer(d, -1)}
+
+    def each_peer(step):
+        each(2, n, step)
+        step(1)
 
     loads = [
         pltpu.make_async_copy(keys_hbm.at[0], kbuf.at[0], local_sem.at[0]),
@@ -133,8 +143,8 @@
             device_id_type=MESH,
         )
 
-    each(1, n, lambda d: k_copy(d).start())
-    each(1, n, lambda d: v_copy(d).start())
+    each_peer(lambda d: k_copy(d).start())
+    each_peer(lambda d: v_copy(d).start())
 
     def places(owner, axis):
         index = lax.broadcasted_iota(jnp.int32, (rows, rows), axis)
@@ -151,7 +161,7 @@
     query_places = places(me, 1)
 
     def score_step(d):
-        owner = lax.rem(me + n - d, n)
+        owner = peer(d, -1)
         bias = jnp.where(places(owner, 0) <= query_places, 0.0, MASKED)
         rows_in = query[...].reshape(wide, depth)
         scores = dot(kbuf[d], rows_in, NT) + jnp.concatenate([bias] * heads, axis=1)

time: 22.5 us -> 21.6 us (0.960)
  Pallas kernels: 19.7 us -> 18.8 us
    pallas_call x1, Pallas kernels: 19.7 us -> 18.8 us  [body(): pl.pallas_call(functools.partial(kernel, n), out_shape=[pltpu.VMEM(query....]
where the time goes in v3:
time: 21.6 us; the launch traced here: 21.4 us
  Pallas kernels  18.8 us (87%)
  local copies, waits for them, and re-layouts  1.96 us (9%)
  between operations  0.64 us (3%)
    pallas_call x1, Pallas kernels, body(): pl.pallas_call(functools.partial(kernel, n), out_shape=[pltpu.VMEM(query....  18.8 us
    unnamed x3, local copies, waits for them, and re-layouts  1.96 us

profile of v3, /device:TPU:0, one launch (start us, length us, event | category | flops | bytes accessed | tf_op | source)
XLA Modules:
  0.0 21.4 jit_solution(13204230821239139701)
XLA Ops:
  0.6 18.8 %shard_map.76 = (f32[4,128,128]{2,1,0:T(8,128)S(1)}, f32[1,128,128]{2,1,0:T(8,128)S(1)}, f32[1,128,128]{2,1,0:T(8,128)S(1)}) custom-call(s32[8]{0:T(128)} %order_ref.1, bf16[4,128,128]{2,1,0:T(8,128)(2,1)} %query_hbm.1, bf16[1,128,128]{2,1,0:T(8,128)(2,1)} %keys_hbm.1, bf16[1,128,128]{2,1,0:T(8,128)(2,1)} %values_hbm.1, bf16[4,128,128]{2,1,0:T(8,128)(2,1)} %ratio_hbm.1), custom_call_target="tpu_custom_call" | custom-call | tf_op jit(solution)/shard_map/pallas_call | solution.py:280
  19.4 0.7 %copy.11 = f32[4,128,128]{2,1,0:T(8,128)} copy(f32[4,128,128]{2,1,0:T(8,128)S(1)} %get-tuple-element.3) | data formatting | bytes 524288
  20.2 0.6 %copy.12 = f32[1,128,128]{2,1,0:T(8,128)} copy(f32[1,128,128]{2,1,0:T(8,128)S(1)} %get-tuple-element.4) | data formatting | bytes 131072
  20.8 0.6 %copy.13 = f32[1,128,128]{2,1,0:T(8,128)} copy(f32[1,128,128]{2,1,0:T(8,128)S(1)} %get-tuple-element.5) | data formatting | bytes 131072

commit v4 on v3

--- a/solution.py
+++ b/solution.py
@@ -36,8 +36,7 @@
     values_hbm,
     ratio_hbm,
     query_rel,
-    key_rel,
-    value_rel,
+    sides,
     query,
     ratio,
     kbuf,
@@ -46,6 +45,7 @@
     grads,
     tops,
     sums,
+    parts,
     low,
     soft,
     dv_out,
@@ -180,6 +180,9 @@
 
     grad_step(0)
 
+    def expect_step(d):
+        parts[d] = jnp.sum(exps[d] * grads[d], axis=0, keepdims=True)
+
     def k_step(d):
         k_copy(d).wait_recv()
         score_step(d)
@@ -206,22 +209,16 @@
     each(1, n, dv_step)
     weight_step(0)
     own_value = value_part(0)
+    expect_step(0)
 
     def v_step(d):
         v_copy(d).wait_recv()
         grad_step(d)
+        expect_step(d)
 
     each(1, n, v_step)
 
-    if n <= 8:
-        expect = sum(jnp.sum(exps[d] * grads[d], axis=0, keepdims=True) for d in range(n))
-    else:
-        expect = lax.fori_loop(
-            0,
-            n,
-            lambda d, e: e + jnp.sum(exps[d] * grads[d], axis=0, keepdims=True),
-            jnp.zeros((1, wide), jnp.float32),
-        )
+    expect = jnp.sum(parts[...], axis=0)
 
     def soft_step(d):
         soft[d] = (exps[d] * (grads[d] - expect)).astype(jnp.bfloat16)
@@ -234,7 +231,7 @@
         dk_out[d] = key_part(d).astype(jnp.bfloat16)
         dk_copy(d).start()
 
-    each(1, n, dk_step)
+    each_peer(dk_step)
     soft_step(0)
     own_key = key_part(0)
 
@@ -250,11 +247,11 @@
         )
 
     each(1, n, lambda d: dv_copy(d).wait_recv())
-    value_rel[0] = vbuf[0].astype(jnp.float32) * (
+    sides[1] = vbuf[0].astype(jnp.float32) * (
         own_value + jnp.sum(dv_in[1:].astype(jnp.float32), axis=0)
     )
     each(1, n, lambda d: dk_copy(d).wait_recv())
-    key_rel[0] = (
+    sides[0] = (
         0.5
         * scale
         * kbuf[0].astype(jnp.float32)
@@ -277,15 +274,14 @@
     anywhere = pl.BlockSpec(memory_space=pl.ANY)
     vmem = pl.BlockSpec(memory_space=pltpu.VMEM)
     dma = pltpu.SemaphoreType.DMA((n,))
-    return pl.pallas_call(
+    query_rel, sides = pl.pallas_call(
         functools.partial(kernel, n),
         out_shape=[
             pltpu.VMEM(query.shape, f32),
-            pltpu.VMEM(keys.shape, f32),
-            pltpu.VMEM(values.shape, f32),
+            pltpu.VMEM((2,) + keys.shape[1:], f32),
         ],
         in_specs=[pl.BlockSpec(memory_space=pltpu.SMEM)] + [anywhere] * 4,
-        out_specs=[vmem] * 3,
+        out_specs=[vmem] * 2,
         scratch_shapes=[
             pltpu.VMEM((heads, rows, depth), bf16),
             pltpu.VMEM((heads, rows, depth), bf16),
@@ -293,6 +289,7 @@
             pltpu.VMEM((n, rows, depth), bf16),
             pltpu.VMEM((n, rows, wide), f32),
             pltpu.VMEM((n, rows, wide), f32),
+            pltpu.VMEM((n, 1, wide), f32),
             pltpu.VMEM((n, 1, wide), f32),
             pltpu.VMEM((n, 1, wide), f32),
             pltpu.VMEM((n, rows, wide), bf16),
@@ -308,6 +305,7 @@
             collective_id=0, has_side_effects=True, vmem_limit_bytes=56 * 2**20
         ),
     )(block_order, query, keys, values, ratio)
+    return query_rel, sides[:1], sides[1:]
 
 
 def solution(mesh):

time: 21.6 us -> 20.8 us (0.963)
  local copies, waits for them, and re-layouts: 1.96 us -> 1.36 us
    unnamed x3 -> x1, local copies, waits for them, and re-layouts: 1.96 us -> 0.71 us
    slice x0 -> x1, local copies, waits for them, and re-layouts: none -> 0.66 us  [body(): return (query_rel, sides[:1], sides[1:])]
where the time goes in v4:
time: 20.8 us; the launch traced here: 20.7 us
  Pallas kernels  18.7 us (90%)
  local copies, waits for them, and re-layouts  1.36 us (7%)
  between operations  0.64 us (3%)
    pallas_call x1, Pallas kernels, body(): pl.pallas_call(functools.partial(kernel, n), out_shape=[pltpu.VMEM(query....  18.7 us
    unnamed x1, local copies, waits for them, and re-layouts  0.71 us
    slice x1, local copies, waits for them, and re-layouts, body(): return (query_rel, sides[:1], sides[1:])  0.66 us

profile of v4, /device:TPU:0, one launch (start us, length us, event | category | flops | bytes accessed | tf_op | source)
XLA Modules:
  0.0 20.7 jit_solution(15615280001073416060)
XLA Ops:
  0.6 18.7 %shard_map.76 = (f32[4,128,128]{2,1,0:T(8,128)S(1)}, f32[2,128,128]{2,1,0:T(8,128)S(1)}) custom-call(s32[8]{0:T(128)} %order_ref.1, bf16[4,128,128]{2,1,0:T(8,128)(2,1)} %query_hbm.1, bf16[1,128,128]{2,1,0:T(8,128)(2,1)} %keys_hbm.1, bf16[1,128,128]{2,1,0:T(8,128)(2,1)} %values_hbm.1, bf16[4,128,128]{2,1,0:T(8,128)(2,1)} %ratio_hbm.1), custom_call_target="tpu_custom_call" | custom-call | tf_op jit(solution)/shard_map/pallas_call | solution.py:277
  19.3 0.7 %copy.9 = f32[4,128,128]{2,1,0:T(8,128)} copy(f32[4,128,128]{2,1,0:T(8,128)S(1)} %get-tuple-element.9) | data formatting | bytes 524288
  20.0 0.7 %fusion = (f32[1,128,128]{2,1,0:T(8,128)}, f32[1,128,128]{2,1,0:T(8,128)}) fusion(f32[2,128,128]{2,1,0:T(8,128)S(1)} %get-tuple-element.6), kind=kLoop, calls=%fused_computation | loop fusion | bytes 262144 | tf_op jit(solution)/shard_map/slice | solution.py:308

commit v5 on v4

--- a/solution.py
+++ b/solution.py
@@ -92,15 +92,15 @@
         pltpu.make_async_copy(ratio_hbm, ratio, local_sem.at[2]),
         pltpu.make_async_copy(values_hbm.at[0], vbuf.at[0], local_sem.at[3]),
     ]
+
+    barrier = pltpu.get_barrier_semaphore()
+
+    def greet(d):
+        pl.semaphore_signal(barrier, inc=1, device_id=to(d), device_id_type=MESH)
+
+    each(1, n, greet)
     for load in loads:
         load.start()
-
-    barrier = pltpu.get_barrier_semaphore()
-
-    def greet(d):
-        pl.semaphore_signal(barrier, inc=1, device_id=to(d), device_id_type=MESH)
-
-    each(1, n, greet)
     pl.semaphore_wait(barrier, n - 1)
 
     def k_copy(d):
@@ -144,7 +144,7 @@
         )
 
     each_peer(lambda d: k_copy(d).start())
-    each_peer(lambda d: v_copy(d).start())
+    each(1, n, lambda d: v_copy(d).start())
 
     def places(owner, axis):
         index = lax.broadcasted_iota(jnp.int32, (rows, rows), axis)

time: 20.8 us -> 20.8 us (level)
  no operation moved by 1% of the time
where the time goes in v5:
time: 20.8 us; the launch traced here: 20.6 us
  Pallas kernels  18.6 us (89%)
  local copies, waits for them, and re-layouts  1.36 us (7%)
  between operations  0.64 us (3%)
    pallas_call x1, Pallas kernels, body(): pl.pallas_call(functools.partial(kernel, n), out_shape=[pltpu.VMEM(query....  18.6 us
    unnamed x1, local copies, waits for them, and re-layouts  0.71 us
    slice x1, local copies, waits for them, and re-layouts, body(): return (query_rel, sides[:1], sides[1:])  0.66 us

profile of v5, /device:TPU:0, one launch (start us, length us, event | category | flops | bytes accessed | tf_op | source)
XLA Modules:
  0.0 20.6 jit_solution(16570106011016325919)
XLA Ops:
  0.6 18.6 %shard_map.76 = (f32[4,128,128]{2,1,0:T(8,128)S(1)}, f32[2,128,128]{2,1,0:T(8,128)S(1)}) custom-call(s32[8]{0:T(128)} %order_ref.1, bf16[4,128,128]{2,1,0:T(8,128)(2,1)} %query_hbm.1, bf16[1,128,128]{2,1,0:T(8,128)(2,1)} %keys_hbm.1, bf16[1,128,128]{2,1,0:T(8,128)(2,1)} %values_hbm.1, bf16[4,128,128]{2,1,0:T(8,128)(2,1)} %ratio_hbm.1), custom_call_target="tpu_custom_call" | custom-call | tf_op jit(solution)/shard_map/pallas_call | solution.py:277
  19.3 0.7 %copy.9 = f32[4,128,128]{2,1,0:T(8,128)} copy(f32[4,128,128]{2,1,0:T(8,128)S(1)} %get-tuple-element.9) | data formatting | bytes 524288
  20.0 0.7 %fusion = (f32[1,128,128]{2,1,0:T(8,128)}, f32[1,128,128]{2,1,0:T(8,128)}) fusion(f32[2,128,128]{2,1,0:T(8,128)S(1)} %get-tuple-element.6), kind=kLoop, calls=%fused_computation | loop fusion | bytes 262144 | tf_op jit(solution)/shard_map/slice | solution.py:308
